TPU v7x, 1024 devices: a whole 4x4x32 slice. The times are simulated.
1024 devices in a mesh: expert: 32 (over z), fsdp: 8 (over x, core), dp: 4 (over y).
Axes of the slice: x: 4, y: 4, z: 32, core: 2. Of those that a mesh axis runs over, the one named last changes fastest.
Arguments:
- out_grad: bfloat16 [20480, 2048], P(('expert', 'fsdp', 'dp')), may hold values from -0.59765625 to 0.59765625
- gates: float32 [20480, 8], P(('expert', 'fsdp', 'dp')), may hold values from 0.02 to 0.6
- routes: int32 [20480, 8], P(('expert', 'fsdp', 'dp')), may hold values from 0 to 63, all different within a row; in each aligned block of 20 rows (0 to 19, 20 to 39, ...) at most 7 rows name the same one
- hidden_acts: bfloat16 [64, 7168, 384], P('expert', ('fsdp', 'dp')), may hold values from -6 to 6
- w_down: bfloat16 [2048, 64, 384], P('fsdp', 'expert'), may hold values from -0.3125 to 0.3125
Outputs:
- hidden_grad: bfloat16 [64, 7168, 384], P('expert', ('fsdp', 'dp'))
- gate_grad: float32 [20480, 8], P(('expert', 'fsdp', 'dp'))
- weight_grad: float32 [2048, 64, 384], P('fsdp', 'expert')
Inputs may be any that keep to these rules, and one draw needn't show every extreme that they name: `routes`: each token names 8 different experts. Among the 20 tokens of one device no expert is named by more than 7 of them, and in every draw some expert is named by exactly 7 tokens of some device.
All inputs are finite; a program needn't handle non-finite values.
Results may differ from a plain program's by a relative error of at most 0.018.
Values may be sent and summed in bfloat16 or wider, within the bound.
A program may use at most 32 MiB of HBM per device.

v0:
```python
import jax
import jax.numpy as jnp
from jax import lax
from jax.sharding import PartitionSpec as P


def shards(out_grad, gates, routes, hidden_acts, w_down):
    n_exp = lax.axis_size("expert")
    exp_dev = w_down.shape[1]
    experts = exp_dev * n_exp
    tok_dev, top_k = routes.shape
    slot_count = hidden_acts.shape[1] // n_exp
    width = out_grad.shape[1]
    flat_routes = routes.reshape(-1)
    onehot = (flat_routes[:, None] == jnp.arange(experts, dtype=jnp.int32)[None, :]).astype(
        jnp.int32
    )
    rank_in = jnp.sum(onehot * (jnp.cumsum(onehot, axis=0) - 1), axis=1)
    slot_pos = (flat_routes % exp_dev * n_exp + flat_routes // exp_dev) * slot_count + rank_in
    buffer_len = experts * slot_count
    token_ids = jnp.arange(flat_routes.shape[0], dtype=jnp.int32) // top_k
    token_of = jnp.full((buffer_len,), -1, jnp.int32).at[slot_pos].set(token_ids)
    gate_buffer = (
        jnp.zeros((buffer_len,), jnp.bfloat16)
        .at[slot_pos]
        .set(gates.reshape(-1).astype(jnp.bfloat16))
    )
    picked = out_grad[jnp.maximum(token_of, 0)]
    send_rows = jnp.where((token_of >= 0)[:, None], picked, jnp.zeros((), jnp.bfloat16))
    routed_rows, routed_gates = (
        lax.all_to_all(
            send_rows.reshape(exp_dev, n_exp, slot_count, width),
            "expert",
            split_axis=1,
            concat_axis=1,
            tiled=True,
        ),
        lax.all_to_all(
            gate_buffer.reshape(exp_dev, n_exp, slot_count),
            "expert",
            split_axis=1,
            concat_axis=1,
            tiled=True,
        ),
    )
    row_count = n_exp * slot_count
    routed_rows = routed_rows.reshape(exp_dev, row_count, width)
    slot_gate = routed_gates.reshape(exp_dev, row_count).astype(jnp.float32)
    w_piece = lax.all_gather(w_down, "fsdp", axis=0, tiled=True)
    back_sum = jnp.einsum("erd,dej->erj", routed_rows, w_piece, preferred_element_type=jnp.float32)
    out_slice = jnp.einsum("erj,dej->erd", hidden_acts, w_piece, preferred_element_type=jnp.float32)
    gate_sum = jnp.sum(routed_rows.astype(jnp.float32) * out_slice, axis=2)
    back_proj, gate_sum = (back_sum, gate_sum)
    hidden_grad = (slot_gate[:, :, None] * back_proj).astype(jnp.bfloat16)
    returned = lax.all_to_all(
        gate_sum.reshape(exp_dev, n_exp, slot_count),
        "expert",
        split_axis=1,
        concat_axis=1,
        tiled=True,
    )
    gate_grad = returned.reshape(-1)[slot_pos].reshape(tok_dev, top_k)
    scaled = (slot_gate[:, :, None] * routed_rows.astype(jnp.float32)).astype(jnp.bfloat16)
    grad_shard = lax.psum_scatter(
        jnp.einsum("erd,erj->dej", scaled, hidden_acts, preferred_element_type=jnp.float32).astype(
            jnp.bfloat16
        ),
        ("fsdp", "dp"),
        scatter_dimension=0,
        tiled=True,
    ).astype(jnp.float32)
    weight_grad = lax.all_gather(grad_shard.astype(jnp.bfloat16), "dp", axis=0, tiled=True).astype(
        grad_shard.dtype
    )
    return (hidden_grad, gate_grad, weight_grad)


def solution(mesh):
    in_specs = (
        P(("expert", "fsdp", "dp"), None),
        P(("expert", "fsdp", "dp"), None),
        P(("expert", "fsdp", "dp"), None),
        P("expert", ("fsdp", "dp"), None),
        P("fsdp", "expert", None),
    )
    out_specs = (
        P("expert", ("fsdp", "dp"), None),
        P(("expert", "fsdp", "dp"), None),
        P("fsdp", "expert", None),
    )
    return jax.shard_map(shards, mesh=mesh, in_specs=in_specs, out_specs=out_specs, check_vma=False)
```

profile of v0, /device:TPU:6, one launch (start us, length us, event | category | flops | bytes accessed | tf_op | source)
XLA Modules:
  0.0 392.0 jit_solution(5030177512838354939)
XLA Ops:
  8.0 0.8 copy.36
  9.1 0.6 reduce-window.6
  9.7 0.2 slice_reduce_fusion
  10.0 0.7 convert_element_type.39
  11.0 1.6 scatter_custom_fusion
  12.5 0.1 reshape.177
  12.7 0.6 copy.41
  13.3 28.7 %all-to-all-start = ((bf16[2,32,7]{2,0,1:T(2,128)(2,1)}), bf16[2,32,7]{2,0,1:T(2,128)(2,1)S(1)}, u32[]{:S(2)}, u32[]{:S(2)}) async-start(bf16[2,32,7]{2,0,1:T(2,128)(2,1)} %copy.41), calls=%async_computation | async-start | bytes 32768 | tf_op jit(solution)/shard_map/all_to_all | solution.py:38
  42.0 1.1 scatter_custom_fusion.1
  43.2 3.2 gather_fusion
  46.4 2.5 gather.9
  49.0 0.1 broadcast_in_dim.32
  49.1 0.2 broadcast_select_fusion
  49.3 3.3 copy.44
  52.7 11.7 %all-to-all-done = bf16[2,32,7]{2,0,1:T(2,128)(2,1)S(1)} async-done(((bf16[2,32,7]{2,0,1:T(2,128)(2,1)}), bf16[2,32,7]{2,0,1:T(2,128)(2,1)S(1)}, u32[]{:S(2)}, u32[]{:S(2)}) %all-to-all-start) | async-done | bytes 928 | tf_op jit(solution)/shard_map/all_to_all | solution.py:38
  64.4 10.3 %all-to-all-start.1 = ((bf16[2,32,7,2048]{3,0,2,1:T(2,128)(2,1)}), bf16[2,32,7,2048]{3,0,2,1:T(2,128)(2,1)S(1)}, u32[]{:S(2)}, u32[]{:S(2)}) async-start(bf16[2,32,7,2048]{3,0,2,1:T(2,128)(2,1)} %copy.44), calls=%async_computation.1 | async-start | bytes 3670016 | tf_op jit(solution)/shard_map/all_to_all | solution.py:31
  74.7 0.8 copy.45
  75.7 0.1 reshape.183
  75.9 168.2 %all-to-all-done.1 = bf16[2,32,7,2048]{3,0,2,1:T(2,128)(2,1)S(1)} async-done(((bf16[2,32,7,2048]{3,0,2,1:T(2,128)(2,1)}), bf16[2,32,7,2048]{3,0,2,1:T(2,128)(2,1)S(1)}, u32[]{:S(2)}, u32[]{:S(2)}) %all-to-all-start.1) | async-done | bytes 1835040 | tf_op jit(solution)/shard_map/all_to_all | solution.py:31
  244.1 3.5 fusion.2
  247.6 3.7 fusion
  251.3 0.1 reshape.179
  251.4 0.6 copy.48
  252.1 10.1 %all-to-all-start.2 = ((f32[2,32,7]{2,0,1:T(2,128)}), f32[2,32,7]{2,0,1:T(2,128)S(1)}, u32[]{:S(2)}, u32[]{:S(2)}) async-start(f32[2,32,7]{2,0,1:T(2,128)} %copy.48), calls=%async_computation.2 | async-start | bytes 65536 | tf_op jit(solution)/shard_map/all_to_all | solution.py:55
  262.1 4.1 %fusion.11 = bf16[2,224,384]{2,1,0:T(8,128)(2,1)} fusion(bf16[2048,2,384]{2,0,1:T(8,128)(2,1)} %all-gather.2.cloned.1.call-done, bf16[2,224,2048]{2,0,1:T(2,128)(2,1)S(1)} %bitcast.23, f32[2,224]{1,0:T(2,128)S(1)} %reshape.183), kind=kOutput, calls=%fused_computation.16 | convolution fusion | flops 704987136 | bytes 5326592 | tf_op jit(solution)/shard_map/erd,dej->erj/dot_general | solution.py:50
  266.3 18.9 %all-to-all-done.2 = f32[2,32,7]{2,0,1:T(2,128)S(1)} async-done(((f32[2,32,7]{2,0,1:T(2,128)}), f32[2,32,7]{2,0,1:T(2,128)S(1)}, u32[]{:S(2)}, u32[]{:S(2)}) %all-to-all-start.2) | async-done | bytes 1824 | tf_op jit(solution)/shard_map/all_to_all | solution.py:55
  285.2 0.1 reshape.180
  285.3 1.6 gather_fusion.1
  287.0 0.7 copy.50
  287.7 82.8 %reduce-scatter.2.cloned.1.call-done = bf16[64,2,384]{2,0,1:T(8,128)(2,1)} async-done(((bf16[2048,2,384]{2,0,1:T(8,128)(2,1)}), bf16[64,2,384]{2,0,1:T(8,128)(2,1)}) %reduce-scatter.2.cloned.1.call-update) | async-done | bytes 98320 | tf_op jit(solution)/shard_map/reduce_scatter | solution.py:64
  370.6 12.7 %all_gather.7 = bf16[256,2,384]{2,0,1:T(8,128)(2,1)S(1)} all-gather(bf16[64,2,384]{2,0,1:T(8,128)(2,1)} %reduce-scatter.2.cloned.1.call-done), channel_id=1, replica_groups=mesh['expert'=32,'fsdp'=8,'dp'=4] {'dp'}, dimensions={0}, use_global_device_ids=true | all-gather | bytes 491520 | tf_op jit(solution)/shard_map/all_gather | solution.py:72
  383.3 1.3 copy.51
  (31 shorter events, 1.0 us)
Async XLA Ops:
  8.0 236.1 %copy-start = (bf16[2,224,384]{2,1,0:T(8,128)(2,1)S(1)}, bf16[2,224,384]{2,1,0:T(8,128)(2,1)}, u32[]{:S(2)}) copy-start(bf16[2,224,384]{2,1,0:T(8,128)(2,1)} %param.8) | copy-start | bytes 1032196
  8.0 35.2 %copy-start.1 = (bf16[20,2048]{1,0:T(8,128)(2,1)S(1)}, bf16[20,2048]{1,0:T(8,128)(2,1)}, u32[]{:S(2)}) copy-start(bf16[20,2048]{1,0:T(8,128)(2,1)} %param.5) | copy-start | bytes 245764
  13.3 51.1 %all-to-all-start = ((bf16[2,32,7]{2,0,1:T(2,128)(2,1)}), bf16[2,32,7]{2,0,1:T(2,128)(2,1)S(1)}, u32[]{:S(2)}, u32[]{:S(2)}) async-start(bf16[2,32,7]{2,0,1:T(2,128)(2,1)} %copy.41), calls=%async_computation | async-start | bytes 32768 | tf_op jit(solution)/shard_map/all_to_all | solution.py:38
  52.7 22.0 %copy-start.2 = (bf16[256,2,384]{2,1,0:T(2,128)(2,1)S(1)}, bf16[256,2,384]{2,1,0:T(2,128)(2,1)}, u32[]{:S(2)}) copy-start(bf16[256,2,384]{2,1,0:T(2,128)(2,1)} %param.9) | copy-start | bytes 1179652
  64.4 179.7 %all-to-all-start.1 = ((bf16[2,32,7,2048]{3,0,2,1:T(2,128)(2,1)}), bf16[2,32,7,2048]{3,0,2,1:T(2,128)(2,1)S(1)}, u32[]{:S(2)}, u32[]{:S(2)}) async-start(bf16[2,32,7,2048]{3,0,2,1:T(2,128)(2,1)} %copy.44), calls=%async_computation.1 | async-start | bytes 3670016 | tf_op jit(solution)/shard_map/all_to_all | solution.py:31
  74.6 173.0 %all-gather.2.cloned.1.call-start = ((), (), s32[]{:S(2)}) async-start(), calls=%async_computation.4 | async-start | bytes 3538944 | tf_op jit(solution)/shard_map/all_gather | solution.py:49
  75.5 295.1 %reduce-scatter.2.cloned.1.call-start = ((), (), s32[]{:S(2)}) async-start(), calls=%async_computation.5 | async-start | bytes 3244032 | tf_op jit(solution)/shard_map/reduce_scatter | solution.py:64
  252.1 33.1 %all-to-all-start.2 = ((f32[2,32,7]{2,0,1:T(2,128)}), f32[2,32,7]{2,0,1:T(2,128)S(1)}, u32[]{:S(2)}, u32[]{:S(2)}) async-start(f32[2,32,7]{2,0,1:T(2,128)} %copy.48), calls=%async_computation.2 | async-start | bytes 65536 | tf_op jit(solution)/shard_map/all_to_all | solution.py:55
Sparse Core Ops, SparseCore 0:
  78.7 45.5 all-gather.1
Sparse Core Ops, SparseCore 1:
  247.7 122.8 reduce-scatter.1
where the time goes:
time: 393 us; the launch traced here: 392 us
  waiting for transfers between devices  282 us (72%)
  starting transfers between devices  49.1 us (12%)
  local copies, waits for them, and re-layouts  19.7 us (5%)
  between operations  15.7 us (4%)
  blocking collectives  12.7 us (3%)
  matrix products  11.3 us (3%)
    all_to_all x1, waiting for transfers between devices, shards(): lax.all_to_all(send_rows.reshape(exp_dev, n_exp, slot_count, width), 'exp...  168 us
    reduce_scatter x1, waiting for transfers between devices, shards(): lax.psum_scatter(jnp.einsum('erd,erj->dej', scaled, hidden_acts, preferre...  82.8 us
    all_to_all x1, starting transfers between devices, shards(): lax.all_to_all(gate_buffer.reshape(exp_dev, n_exp, slot_count), 'expert',...  28.7 us
    all_to_all x1, waiting for transfers between devices, shards(): lax.all_to_all(gate_sum.reshape(exp_dev, n_exp, slot_count), 'expert', sp...  18.9 us
    all_gather x1, blocking collectives, shards(): lax.all_gather(grad_shard.astype(jnp.bfloat16), 'dp', axis=0, tiled=True)  12.7 us
    all_to_all x1, waiting for transfers between devices, shards(): lax.all_to_all(gate_buffer.reshape(exp_dev, n_exp, slot_count), 'expert',...  11.7 us
    all_to_all x1, starting transfers between devices, shards(): lax.all_to_all(send_rows.reshape(exp_dev, n_exp, slot_count, width), 'exp...  10.3 us
    all_to_all x1, starting transfers between devices, shards(): lax.all_to_all(gate_sum.reshape(exp_dev, n_exp, slot_count), 'expert', sp...  10.1 us
  transfers between devices with their start and end apart: 5, of which 4 were waited for; matrix products, arithmetic and copies ran while one was open for 7% of the time, Pallas kernels for 0%

commit v1 on v0

v1 whole, which is shorter than its diff:
```python
import functools

import jax
import jax.numpy as jnp
from jax import lax
from jax.experimental import pallas as pl
from jax.experimental.pallas import tpu as pltpu
from jax.sharding import PartitionSpec as P

MESH = pl.DeviceIdType.MESH
F32 = jnp.float32
BF16 = jnp.bfloat16
LANES = 128
RPAD = 8
CODE_SHIFT = 256.0
LAG = 3
PIECES = 3


def remote(src, dst, send, recv, where):
    return pltpu.make_async_remote_copy(
        src_ref=src, dst_ref=dst, send_sem=send, recv_sem=recv, device_id=where, device_id_type=MESH
    )


def kernel(
    n_e, n_x, n_p, tok,
    pre, hp, wt, code, hg_out, gg_out, wg_out,
    blk, xr, hidr, w2, spread, tgt, lanemask, p_send, p_recv, scaled_rows, gate_cols, acc,
    gs, gr, ws, wc, wd, wr, wag,
    x_send, x_recv, h_send, h_recv, w_send, w_recv, loc,
    z_send, z_recv, ps_send, ps_recv, g_send, g_recv, c_send, c_recv, r_send, r_recv, a_send, a_recv,
):
    me = lax.axis_index("expert")
    f = lax.axis_index("fsdp")
    p = lax.axis_index("dp")
    xi, core = f // 2, f % 2
    half = n_e // 2
    piece_rows = pre.shape[1] - 16
    og_rows = n_x * piece_rows
    blk_rows = og_rows + 16
    q_n = piece_rows // tok
    chunk = blk_rows // PIECES
    width = hp.shape[2]
    fs = wt.shape[1]
    rows_x = n_x * RPAD
    right, left = (me + 1) % n_e, (me + n_e - 1) % n_e

    def x_dev(t):
        return {"fsdp": t * 2 + core}

    other = {"fsdp": xi * 2 + 1 - core}

    barrier = pltpu.get_barrier_semaphore()

    @pl.loop(1, n_e)
    def _(o):
        pl.semaphore_signal(barrier, inc=1, device_id={"expert": (me + o) % n_e}, device_id_type=MESH)

    for o in range(1, n_x):
        pl.semaphore_signal(barrier, inc=1, device_id=x_dev((xi + o) % n_x), device_id_type=MESH)
    pl.semaphore_signal(barrier, inc=1, device_id=other, device_id_type=MESH)
    for o in range(1, n_p):
        pl.semaphore_signal(barrier, inc=1, device_id={"dp": (p + o) % n_p}, device_id_type=MESH)
    pl.semaphore_wait(barrier, (n_e - 1) + (n_x - 1) + 1 + (n_p - 1))

    def x_copy(o):
        t = (xi + o) % n_x
        return remote(pre.at[t], xr.at[xi], x_send.at[o - 1], x_recv.at[o - 1], x_dev(t))

    def h_copy(o):
        t = (xi + o) % n_x
        return remote(hp, hidr.at[xi], h_send.at[o - 1], h_recv.at[o - 1], x_dev(t))

    w_copy = remote(wt, w2.at[core], w_send, w_recv, other)
    own_w = pltpu.make_async_copy(wt, w2.at[core], loc.at[0])
    own_h = pltpu.make_async_copy(hp, hidr.at[xi], loc.at[1])
    own_x = pltpu.make_async_copy(pre.at[xi], xr.at[xi], loc.at[2])

    for o in range(1, n_x):
        x_copy(o).start()
    own_x.start()
    w_copy.start()
    for o in range(1, n_x):
        h_copy(o).start()
    own_w.start()
    own_h.start()

    k_tok = lax.broadcasted_iota(jnp.int32, spread.shape, 0)
    lane = lax.broadcasted_iota(jnp.int32, spread.shape, 1)
    token_of = lane // piece_rows * tok + lane % tok
    spread[...] = jnp.where((token_of == k_tok) & (lane < og_rows), 1.0, 0.0).astype(BF16)
    row = lax.broadcasted_iota(jnp.int32, tgt.shape, 0)
    col = lax.broadcasted_iota(jnp.int32, tgt.shape, 1)
    expert_row = me * 2 + row // rows_x
    tgt[...] = (expert_row * RPAD + row % RPAD).astype(F32) - CODE_SHIFT
    lanemask[...] = jnp.where(col // tok == row // RPAD % n_x, 1.0, 0.0)
    acc[...] = jnp.zeros_like(acc)
    gs[...] = jnp.zeros_like(gs)

    own_x.wait()
    for o in range(1, n_x):
        x_copy(o).wait_recv()
    table = jnp.zeros((16, LANES), F32)
    for x in range(n_x):
        blk[me, x * piece_rows : (x + 1) * piece_rows, :] = xr[x, :piece_rows, :]
        table = table + xr[x, piece_rows:, :].astype(F32)
    blk[me, og_rows:, :] = table.astype(BF16)

    def z_copy(way, step, c):
        slot = (me + n_e - step) % n_e if way == 0 else (me + step) % n_e
        ref = blk.at[slot, pl.ds(c * chunk, chunk), :]
        to = right if way == 0 else left
        return remote(ref, ref, z_send.at[way, step, c], z_recv.at[way, step, c], {"expert": to})

    def z_arrival(way, step, c):
        slot = (me + n_e - step - 1) % n_e if way == 0 else (me + step + 1) % n_e
        ref = blk.at[slot, pl.ds(c * chunk, chunk), :]
        to = right if way == 0 else left
        return remote(ref, ref, z_send.at[way, step, c], z_recv.at[way, step, c], {"expert": to})

    for c in range(PIECES):
        z_copy(0, 0, c).start()
        z_copy(1, 0, c).start()

    own_w.wait()
    w_copy.wait_recv()

    def block_rows(e, i, ab):
        routing = blk[e, og_rows:, :].astype(F32)
        codes, gates = routing[:8], routing[8:]
        want, mask = tgt[...], lanemask[...]
        hit = jnp.zeros(tgt.shape, F32)
        gate = jnp.zeros(tgt.shape, F32)
        for k in range(8):
            same = codes[k : k + 1, :] == want
            hit = jnp.where(same, 1.0, hit)
            gate = jnp.where(same, gates[k : k + 1, :], gate)
        gate_col = jnp.sum(gate * mask, axis=1, keepdims=True)
        gate_cols[i, ab] = jnp.broadcast_to(gate_col, tgt.shape)
        wide = jnp.dot((hit * mask).astype(BF16), spread[...], preferred_element_type=F32)
        q_of = lax.broadcasted_iota(jnp.int32, (1, blk_rows), 1) % piece_rows // tok
        pick = jnp.concatenate(
            [jnp.where(q_of == q, wide, 0.0).astype(BF16) for q in range(q_n)], axis=0
        )
        got = jnp.dot(pick, blk[e], preferred_element_type=F32)
        got = jnp.concatenate(
            [got[q * 2 * rows_x : (q + 1) * 2 * rows_x] for q in range(q_n)], axis=1
        )
        return got.astype(BF16), (got * gate_col).astype(BF16)

    def compute(i):
        ea, eb = (me + i) % n_e, (me + n_e - i - 1) % n_e
        rows_a, scaled_a = block_rows(ea, i, 0)
        rows_b, scaled_b = block_rows(eb, i, 1)
        parts = []
        for x in range(2):
            cut = slice(x * rows_x, (x + 1) * rows_x)
            scaled_rows[x, i, :rows_x, :] = scaled_a[cut]
            scaled_rows[x, i, rows_x:, :] = scaled_b[cut]
            lhs = jnp.concatenate([rows_a[cut], rows_b[cut]], axis=0)
            parts.append(
                jnp.dot(lhs[:, :fs], w2[0, x], preferred_element_type=F32)
                + jnp.dot(lhs[:, fs:], w2[1, x], preferred_element_type=F32)
            )
        for x in range(n_x):
            tiles = [
                parts[b][ab * rows_x + x * RPAD : ab * rows_x + (x + 1) * RPAD]
                for ab in range(2)
                for b in range(2)
            ]
            p_send[x, i] = jnp.concatenate(tiles, axis=0).astype(BF16)

    def p_copy(o, i):
        t = (xi + o) % n_x
        return remote(
            p_send.at[t, i], p_recv.at[xi, i], ps_send.at[o - 1, i], ps_recv.at[o - 1, i], x_dev(t)
        )

    def combine(i):
        for o in range(1, n_x):
            p_copy(o, i).wait_recv()
        total = p_send[xi, i].astype(F32)
        for o in range(1, n_x):
            total = total + p_recv[(xi + n_x - o) % n_x, i].astype(F32)
        for ab in range(2):
            e = (me + i) % n_e if ab == 0 else (me + n_e - i - 1) % n_e
            part = total[ab * 16 : (ab + 1) * 16]
            gate = jnp.concatenate(
                [gate_cols[i, ab, pl.ds(pl.multiple_of(x * rows_x + xi * RPAD, RPAD), RPAD), :] for x in range(2)],
                axis=0,
            )
            hg_out[e] = (gate[:, :1] * part).astype(BF16)
            grad = jnp.sum(part * hp[e].astype(F32), axis=1, keepdims=True)
            r16 = lax.broadcasted_iota(jnp.int32, (16, LANES), 0)
            l16 = lax.broadcasted_iota(jnp.int32, (16, LANES), 1)
            line = jnp.where(l16 == e % 8 * 16 + r16, grad, 0.0)
            gs[e // 8] += jnp.sum(line, axis=0, keepdims=True)

    def grad_step(j):
        for x in range(2):
            lhs, rhs = [], []
            for u in range(2):
                i = 2 * j + u
                lhs.append(scaled_rows[x, i])
                for ab in range(2):
                    e = (me + i) % n_e if ab == 0 else (me + n_e - i - 1) % n_e
                    for s in range(n_x):
                        rhs.append(hidr[s, e].astype(F32)[x * RPAD : (x + 1) * RPAD])
            lhs = jnp.concatenate(lhs, axis=0)
            rhs = jnp.concatenate(rhs, axis=0).astype(BF16)
            acc[x] += lax.dot_general(lhs, rhs, (((0,), (0,)), ((), ())), preferred_element_type=F32)

    @pl.loop(0, half)
    def _(i):
        for c in range(PIECES):
            z_arrival(0, i, c).wait_recv()

            @pl.when(i < half - 1)
            def _():
                z_copy(0, i + 1, c).start()

            @pl.when(i >= 1)
            def _():
                z_arrival(1, i - 1, c).wait_recv()

            @pl.when((i >= 1) & (i < half - 1))
            def _():
                z_copy(1, i, c).start()

        compute(i)
        for o in range(1, n_x):
            p_copy(o, i).start()

        @pl.when(i >= LAG)
        def _():
            combine(i - LAG)

        @pl.when(i == half // 2)
        def _():
            own_h.wait()
            for o in range(1, n_x):
                h_copy(o).wait_recv()

        @pl.when(i >= half // 2)
        def _():
            grad_step(i - half // 2)

    cut = fs // n_p
    for x in range(2):
        ws[x] = acc[x, pl.ds(pl.multiple_of((1 - core) * fs, fs), fs), :].astype(BF16)
    c_copy = remote(ws, wc, c_send, c_recv, other)
    c_copy.start()

    @pl.loop(half - LAG, half)
    def _(i):
        combine(i)

    gr[me] = gs[me // 8]

    def g_copy(o):
        t = (me + o) % n_e
        return remote(gs.at[t // 8], gr.at[me], g_send.at[o], g_recv.at[o], {"expert": t})

    @pl.loop(1, n_e)
    def _(o):
        g_copy(o).start()

    c_copy.wait_recv()

    def r_copy(o):
        t = (p + o) % n_p
        return remote(wd.at[t], wr.at[p], r_send.at[o - 1], r_recv.at[o - 1], {"dp": t})

    def summed(t, x):
        at = pl.multiple_of(core * fs + t * cut, cut)
        return acc[x, pl.ds(at, cut), :] + wc[x, pl.ds(pl.multiple_of(t * cut, cut), cut), :].astype(F32)

    for o in range(1, n_p):
        t = (p + o) % n_p
        for x in range(2):
            wd[t, x] = summed(t, x).astype(BF16)
        r_copy(o).start()

    @pl.loop(1, n_e)
    def _(o):
        g_copy(o).wait_recv()

    mine = [summed(p, x) for x in range(2)]
    for o in range(1, n_p):
        r_copy(o).wait_recv()
    for x in range(2):
        for o in range(1, n_p):
            mine[x] = mine[x] + wr[(p + n_p - o) % n_p, x].astype(F32)
        wag[p, x] = mine[x].astype(BF16)

    def a_copy(o):
        t = (p + o) % n_p
        return remote(wag.at[p], wag.at[p], a_send.at[o - 1], a_recv.at[o - 1], {"dp": t})

    def a_arrival(o):
        s = (p + n_p - o) % n_p
        return remote(
            wag.at[s], wag.at[s], a_send.at[o - 1], a_recv.at[o - 1], {"dp": (p + o) % n_p}
        )

    for o in range(1, n_p):
        a_copy(o).start()

    pairs = code[...]
    e_of = lax.broadcasted_iota(jnp.int32, (pairs.shape[0], n_e), 1)
    one = jnp.where(e_of == pairs // 16, 1.0, 0.0)
    got = jnp.dot(
        one, gr[:, 0, :], preferred_element_type=F32, precision=lax.Precision.HIGHEST
    )
    l_of = lax.broadcasted_iota(jnp.int32, got.shape, 1)
    gg_out[...] = jnp.sum(
        jnp.where(l_of == me % 8 * 16 + pairs % 16, got, 0.0), axis=1, keepdims=True
    )

    for o in range(1, n_p):
        a_arrival(o).wait_recv()
    for t in range(n_p):
        for x in range(2):
            wg_out[x, t * cut : (t + 1) * cut, :] = wag[t, x].astype(F32)

    for o in range(1, n_x):
        x_copy(o).wait_send()
        h_copy(o).wait_send()
    w_copy.wait_send()
    c_copy.wait_send()
    for o in range(1, n_p):
        r_copy(o).wait_send()
        a_copy(o).wait_send()

    @pl.loop(1, n_e)
    def _(o):
        g_copy(o).wait_send()

    @pl.loop(0, half)
    def _(i):
        for o in range(1, n_x):
            p_copy(o, i).wait_send()
        for c in range(PIECES):
            z_copy(0, i, c).wait_send()

            @pl.when(i < half - 1)
            def _():
                z_copy(1, i, c).wait_send()


def shards(n_e, n_x, n_p, out_grad, gates, routes, hidden_acts, w_down):
    tok, top = routes.shape
    exp_dev = w_down.shape[1]
    fs = w_down.shape[0]
    width = w_down.shape[2]
    slot = hidden_acts.shape[1] // n_e
    half = n_e // 2
    chip_cols = 2 * fs
    q_n = chip_cols // LANES
    piece_rows = q_n * tok
    blk_rows = n_x * piece_rows + 16
    rows_x = n_x * RPAD
    xi = lax.axis_index("fsdp") // 2

    earlier = jnp.arange(tok)[:, None] > jnp.arange(tok)[None, :]
    same = routes[:, :, None, None] == routes[None, None, :, :]
    rank = jnp.sum((same & earlier[:, None, :, None]).astype(jnp.int32), axis=(2, 3))
    code = routes * RPAD + rank
    table = jnp.concatenate(
        [(code.T.astype(F32) - CODE_SHIFT).astype(BF16), gates.T.astype(BF16)], axis=0
    )
    table = jnp.concatenate([table] * n_x, axis=1)
    table = jnp.pad(table, ((0, 0), (0, LANES - n_x * tok)))
    lane = jnp.arange(LANES, dtype=jnp.int32)
    table = jnp.where((lane // tok == xi)[None, :], table, jnp.zeros((), BF16))
    pieces = out_grad.reshape(tok, n_x, q_n, LANES).transpose(1, 2, 0, 3).reshape(n_x, piece_rows, LANES)
    pre = jnp.concatenate([pieces, jnp.broadcast_to(table[None], (n_x, 16, LANES))], axis=1)
    hp = hidden_acts.reshape(exp_dev, n_e, slot, width).transpose(1, 0, 2, 3)
    hp = jnp.pad(hp, ((0, 0), (0, 0), (0, RPAD - slot), (0, 0))).reshape(n_e, 2 * RPAD, width)
    wt = w_down.transpose(1, 0, 2)

    dma = pltpu.SemaphoreType.DMA
    vmem = pl.BlockSpec(memory_space=pltpu.VMEM)
    cut = fs // n_p
    hg, gg, wg = pl.pallas_call(
        functools.partial(kernel, n_e, n_x, n_p, tok),
        out_shape=(
            jax.ShapeDtypeStruct((n_e, 2 * RPAD, width), BF16),
            jax.ShapeDtypeStruct((tok * top, 1), F32),
            jax.ShapeDtypeStruct((exp_dev, fs, width), F32),
        ),
        in_specs=[vmem] * 4,
        out_specs=(vmem,) * 3,
        scratch_shapes=[
            pltpu.VMEM((n_e, blk_rows, LANES), BF16),
            pltpu.VMEM((n_x, piece_rows + 16, LANES), BF16),
            pltpu.VMEM((n_x, n_e, 2 * RPAD, width), BF16),
            pltpu.VMEM((2, exp_dev, fs, width), BF16),
            pltpu.VMEM((LANES, blk_rows), BF16),
            pltpu.VMEM((2 * rows_x, LANES), F32),
            pltpu.VMEM((2 * rows_x, LANES), F32),
            pltpu.VMEM((n_x, half, 4 * RPAD, width), BF16),
            pltpu.VMEM((n_x, half, 4 * RPAD, width), BF16),
            pltpu.VMEM((2, half, 2 * rows_x, chip_cols), BF16),
            pltpu.VMEM((half, 2, 2 * rows_x, LANES), F32),
            pltpu.VMEM((2, chip_cols, width), F32),
            pltpu.VMEM((n_e // 8, 1, LANES), F32),
            pltpu.VMEM((n_e, 1, LANES), F32),
            pltpu.VMEM((2, fs, width), BF16),
            pltpu.VMEM((2, fs, width), BF16),
            pltpu.VMEM((n_p, 2, cut, width), BF16),
            pltpu.VMEM((n_p, 2, cut, width), BF16),
            pltpu.VMEM((n_p, 2, cut, width), BF16),
            dma((n_x - 1,)), dma((n_x - 1,)), dma((n_x - 1,)), dma((n_x - 1,)), dma, dma, dma((3,)),
            dma((2, half, PIECES)), dma((2, half, PIECES)),
            dma((n_x - 1, half)), dma((n_x - 1, half)),
            dma((n_e,)), dma((n_e,)), dma, dma,
            dma((n_p - 1,)), dma((n_p - 1,)), dma((n_p - 1,)), dma((n_p - 1,)),
        ],
        compiler_params=pltpu.CompilerParams(
            collective_id=0, has_side_effects=True, vmem_limit_bytes=40 * 1024 * 1024
        ),
    )(pre, hp, wt, code.reshape(tok * top, 1))
    hg = hg.reshape(n_e, exp_dev, RPAD, width)[:, :, :slot].transpose(1, 0, 2, 3)
    return hg.reshape(exp_dev, n_e * slot, width), gg.reshape(tok, top), wg.transpose(1, 0, 2)


def solution(mesh):
    n_x = mesh.shape["fsdp"] // 2
    in_specs = (
        P(("expert", "fsdp", "dp"), None),
        P(("expert", "fsdp", "dp"), None),
        P(("expert", "fsdp", "dp"), None),
        P("expert", ("fsdp", "dp"), None),
        P("fsdp", "expert", None),
    )
    out_specs = (
        P("expert", ("fsdp", "dp"), None),
        P(("expert", "fsdp", "dp"), None),
        P("fsdp", "expert", None),
    )
    return jax.shard_map(
        functools.partial(shards, mesh.shape["expert"], n_x, mesh.shape["dp"]),
        mesh=mesh,
        in_specs=in_specs,
        out_specs=out_specs,
        check_vma=False,
    )
```

time: 393 us -> 129 us (0.33)
  waiting for transfers between devices: 282 us -> 0 us
  Pallas kernels: 0 us -> 118 us
  starting transfers between devices: 49.1 us -> 0 us
  between operations: 15.7 us -> 0.77 us
  blocking collectives: 12.7 us -> 0 us
  local copies, waits for them, and re-layouts: 19.7 us -> 7.12 us
  matrix products: 11.3 us -> 0 us
    all_to_all x3 -> x0, waiting for transfers between devices: 199 us -> none  [the longest x1 168 us: shards(): lax.all_to_all(send_rows.reshape(exp_dev, n_exp, slot_count, width), 'exp...]
    pallas_call x0 -> x1, Pallas kernels: none -> 118 us  [shards(): pl.pallas_call(functools.partial(kernel, n_e, n_x, n_p, tok), out_shape=(...]
    reduce_scatter x1 -> x0, waiting for transfers between devices: 82.8 us -> none  [shards(): lax.psum_scatter(jnp.einsum('erd,erj->dej', scaled, hidden_acts, preferre...]
    all_to_all x3 -> x0, starting transfers between devices: 49.1 us -> none  [the longest x1 28.7 us: shards(): lax.all_to_all(gate_buffer.reshape(exp_dev, n_exp, slot_count), 'expert',...]
    all_gather x1 -> x0, blocking collectives: 12.7 us -> none  [shards(): lax.all_gather(grad_shard.astype(jnp.bfloat16), 'dp', axis=0, tiled=True)]
    dot_general x3 -> x0, matrix products: 11.3 us -> none  [the longest x1 4.11 us: shards(): jnp.einsum('erd,dej->erj', routed_rows, w_piece, preferred_element_type=j...]
    gather x3 -> x0, local copies, waits for them, and re-layouts: 7.38 us -> none  [the longest x2 5.77 us: shards(): picked = out_grad[jnp.maximum(token_of, 0)]]
  transfers between devices with their start and end apart: 5 -> 0, of which waited for: 4 -> 0; matrix products, arithmetic and copies ran while one was open for 7% -> 0% of each run, Pallas kernels for 0% -> 0%
where the time goes in v1:
time: 129 us
  Pallas kernels  118 us (91%)
  local copies, waits for them, and re-layouts  7.12 us (6%)
  other arithmetic  3.38 us (3%)
    pallas_call x1, Pallas kernels, shards(): pl.pallas_call(functools.partial(kernel, n_e, n_x, n_p, tok), out_shape=(...  118 us
    unnamed x18, local copies, waits for them, and re-layouts  6.63 us
    reduce_sum x1, other arithmetic, shards(): jnp.sum((same & earlier[:, None, :, None]).astype(jnp.int32), axis=(2, 3))  3.16 us

profile of v1, /device:TPU:6, one launch (start us, length us, event | category | flops | bytes accessed | tf_op | source)
XLA Modules:
  0.0 129.1 jit_solution(15578337760635549539)
XLA Ops:
  0.6 0.0 copy-start.3
  0.7 0.6 copy-done.3
  1.3 0.1 copy.62
  1.4 0.0 copy-start.4
  1.4 3.2 %convert_reduce_fusion = s32[20,8]{1,0:T(8,128)S(1)} fusion(s32[20,8]{0,1:T(8,128)S(1)} %copy-done.3, s32[20,8]{1,0:T(8,128)S(1)} %copy.62, pred[20,20]{1,0:T(8,128)(4,1)S(1)} %iota_compare_fusion), kind=kLoop, calls=%fused_computation | loop fusion | flops 102240 | bytes 2320 | tf_op jit(solution)/shard_map/reduce_sum | solution.py:368
  4.6 0.0 copy-start.2
  4.6 0.1 copy.63
  4.7 0.0 copy-done.4
  4.7 0.1 fusion.12
  4.8 0.1 copy.68
  4.9 0.1 reshape.67.code
  5.0 0.5 copy-done.2
  5.5 0.0 copy-start.1
  5.6 0.9 copy-done.1
  6.5 0.3 copy.65
  6.7 0.1 copy.75
  6.8 0.0 copy-start
  6.8 0.1 pad_bitcast_fusion.hp
  6.9 0.9 copy-done
  7.8 117.8 %shard_map.76 = (bf16[32,16,384]{2,1,0:T(8,128)(2,1)S(1)}, f32[160,1]{1,0:T(8,128)S(1)}, f32[2,256,384]{2,1,0:T(8,128)S(1)}) custom-call(bf16[4,96,128]{2,1,0:T(8,128)(2,1)S(1)} %pad_maximum_fusion.pre, bf16[32,16,384]{2,1,0:T(8,128)(2,1)S(1)} %pad_bitcast_fusion.hp, bf16[2,256,384]{2,1,0:T(8,128)(2,1)S(1)} %bitcast.21, s32[160,1]{1,0:T(8,128)S(1)} %reshape.67.code), custom_call_target="tpu_custom_call" | custom-call | tf_op jit(solution)/shard_map/pallas_call | solution.py:386
  125.7 0.3 copy.74
  126.0 0.8 copy.71
  126.7 0.1 reduce
  126.8 0.1 reshape.66
  126.9 0.7 copy.72
  127.6 1.5 %copy.73 = f32[256,2,384]{2,1,0:T(2,128)} copy(f32[256,2,384]{2,0,1:T(8,128)S(1)} %bitcast.22) | data formatting | bytes 1572864
  (9 shorter events, 0.2 us)
Async XLA Ops:
  0.6 0.7 copy-start.3
  1.4 3.3 %copy-start.4 = (f32[20,8]{0,1:T(8,128)S(1)}, f32[20,8]{0,1:T(8,128)}, u32[]{:S(2)}) copy-start(f32[20,8]{0,1:T(8,128)} %param.6) | copy-start | bytes 1924
  4.6 0.9 copy-start.2
  5.5 1.0 copy-start.1
  6.8 1.0 copy-start

commit v2 on v1

v2 whole, which is shorter than its diff:
```python
import functools

import jax
import jax.numpy as jnp
from jax import lax
from jax.experimental import pallas as pl
from jax.experimental.pallas import tpu as pltpu
from jax.sharding import PartitionSpec as P

MESH = pl.DeviceIdType.MESH
F32 = jnp.float32
BF16 = jnp.bfloat16
LANES = 128
RPAD = 8
CODE_SHIFT = 256.0
PIECES = 3
JUMP = 6


def remote(src, dst, send, recv, where):
    return pltpu.make_async_remote_copy(
        src_ref=src, dst_ref=dst, send_sem=send, recv_sem=recv, device_id=where, device_id_type=MESH
    )


def kernel(
    n_e, n_x, n_p, tok,
    pre, routes, gates, hp, wt, hg_out, gg_out, wg_out,
    blk, xr, tile, tr, codes_own, hidr, w2, spread, tgt, lanemask, p_send, p_recv, scaled_rows, gate_cols, acc,
    gs, gr, ws, wc, wd, wr, wag,
    x_send, x_recv, t_send, t_recv, h_send, h_recv, w_send, w_recv, loc,
    z_send, z_recv, ps_send, ps_recv, g_send, g_recv, c_send, c_recv, r_send, r_recv, a_send, a_recv,
):
    me = lax.axis_index("expert")
    f = lax.axis_index("fsdp")
    p = lax.axis_index("dp")
    xi, core = f // 2, f % 2
    half = n_e // 2
    piece_rows = pre.shape[1]
    og_rows = n_x * piece_rows
    blk_rows = og_rows + 16
    q_n = piece_rows // tok
    chunk = blk_rows // PIECES
    width = hp.shape[2]
    fs = wt.shape[1]
    rows_x = n_x * RPAD

    def x_dev(t):
        return {"fsdp": t * 2 + core}

    other = {"fsdp": xi * 2 + 1 - core}

    barrier = pltpu.get_barrier_semaphore()

    for o in (1, n_e - 1, JUMP, n_e - JUMP):
        pl.semaphore_signal(barrier, inc=1, device_id={"expert": (me + o) % n_e}, device_id_type=MESH)
    for o in range(1, n_x):
        pl.semaphore_signal(barrier, inc=1, device_id=x_dev((xi + o) % n_x), device_id_type=MESH)
    pl.semaphore_signal(barrier, inc=1, device_id=other, device_id_type=MESH)
    for o in range(1, n_p):
        pl.semaphore_signal(barrier, inc=1, device_id={"dp": (p + o) % n_p}, device_id_type=MESH)
    pl.semaphore_wait(barrier, 4 + (n_x - 1) + 1 + (n_p - 1))

    def x_copy(o):
        t = (xi + o) % n_x
        return remote(pre.at[t], xr.at[xi], x_send.at[o - 1], x_recv.at[o - 1], x_dev(t))

    def t_copy(o):
        t = (xi + o) % n_x
        return remote(tile, tr.at[xi], t_send.at[o - 1], t_recv.at[o - 1], x_dev(t))

    def h_copy(o):
        t = (xi + o) % n_x
        return remote(hp, hidr.at[xi], h_send.at[o - 1], h_recv.at[o - 1], x_dev(t))

    w_copy = remote(wt, w2.at[core], w_send, w_recv, other)
    own_w = pltpu.make_async_copy(wt, w2.at[core], loc.at[0])
    own_h = pltpu.make_async_copy(hp, hidr.at[xi], loc.at[1])
    own_x = pltpu.make_async_copy(pre.at[xi], xr.at[xi], loc.at[2])

    for o in range(1, n_x):
        x_copy(o).start()
    own_x.start()
    w_copy.start()
    own_w.start()
    own_h.start()

    t_row = lax.broadcasted_iota(jnp.int32, (tok, LANES), 0)
    t_col = lax.broadcasted_iota(jnp.int32, (tok, LANES), 1)
    place = jnp.where(t_col == xi * tok + t_row, 1.0, 0.0)
    both = jnp.concatenate(
        [routes[...].astype(F32), gates[...].astype(BF16).astype(F32)], axis=0
    ).astype(BF16)
    placed = jnp.dot(both, place.astype(BF16), preferred_element_type=F32)
    own_lane = lax.broadcasted_iota(jnp.int32, (1, LANES), 1) // tok == xi
    expert = lax.broadcasted_iota(jnp.int32, (2 * n_e, LANES), 0).astype(F32)
    named = jnp.zeros((2 * n_e, LANES), F32)
    for k in range(8):
        named = jnp.where((placed[k : k + 1] == expert) & own_lane, 1.0, named)
    l_row = lax.broadcasted_iota(jnp.int32, (LANES, LANES), 0)
    l_col = lax.broadcasted_iota(jnp.int32, (LANES, LANES), 1)
    before = jnp.where(l_row < l_col, 1.0, 0.0).astype(BF16)
    count = jnp.dot(named.astype(BF16), before, preferred_element_type=F32)
    ranks = [
        jnp.sum(jnp.where(placed[k : k + 1] == expert, count, 0.0), axis=0, keepdims=True)
        for k in range(8)
    ]
    own_codes = placed[:8] * RPAD + jnp.concatenate(ranks, axis=0)
    codes_own[...] = own_codes
    tile[...] = jnp.concatenate(
        [jnp.where(own_lane, own_codes - CODE_SHIFT, 0.0), placed[8:]], axis=0
    ).astype(BF16)
    for o in range(1, n_x):
        t_copy(o).start()
    tr[xi] = tile[...]
    for o in range(1, n_x):
        h_copy(o).start()

    k_tok = lax.broadcasted_iota(jnp.int32, spread.shape, 0)
    lane = lax.broadcasted_iota(jnp.int32, spread.shape, 1)
    token_of = lane // piece_rows * tok + lane % tok
    spread[...] = jnp.where((token_of == k_tok) & (lane < og_rows), 1.0, 0.0).astype(BF16)
    row = lax.broadcasted_iota(jnp.int32, tgt.shape, 0)
    col = lax.broadcasted_iota(jnp.int32, tgt.shape, 1)
    expert_row = me * 2 + row // rows_x
    tgt[...] = (expert_row * RPAD + row % RPAD).astype(F32) - CODE_SHIFT
    lanemask[...] = jnp.where(col // tok == row // RPAD % n_x, 1.0, 0.0)
    acc[...] = jnp.zeros_like(acc)

    own_x.wait()
    for o in range(1, n_x):
        x_copy(o).wait_recv()
        t_copy(o).wait_recv()
    table = jnp.zeros((16, LANES), F32)
    for x in range(n_x):
        blk[me, x * piece_rows : (x + 1) * piece_rows, :] = xr[x]
        table = table + tr[x].astype(F32)
    blk[me, og_rows:, :] = table.astype(BF16)

    def hop(way, slot, dist, c, stride):
        ref = blk.at[slot, pl.ds(c * chunk, chunk), :]
        to = (me + stride) % n_e if way == 0 else (me + n_e - stride) % n_e
        return remote(ref, ref, z_send.at[way, dist - 1, c], z_recv.at[way, dist - 1, c], {"expert": to})

    def seen(way, dist):
        return (me + n_e - dist) % n_e if way == 0 else (me + dist) % n_e

    def order(i):
        mid = jnp.where(i % 2 == 0, JUMP - 1 + i // 2, (i + 3) // 2)
        return jnp.where((i < 2) | (i >= 2 * JUMP - 4), i + 1, mid)

    for c in range(PIECES):
        for way in range(2):
            hop(way, me, 1, c, 1).start()
    for c in range(PIECES):
        for way in range(2):
            hop(way, me, JUMP, c, JUMP).start()

    def pass_on(way, dist, c, last):
        hop(way, seen(way, dist), dist, c, 1).wait_recv()

        @pl.when((dist != JUMP - 1) & (dist != last))
        def _():
            hop(way, seen(way, dist), dist + 1, c, 1).start()

    def pair(i):
        far = jnp.where(i >= 1, order(jnp.maximum(i - 1, 0)), 0)
        return seen(1, far), seen(0, order(i))

    own_w.wait()
    w_copy.wait_recv()

    def block_rows(e, i, ab):
        routing = blk[e, og_rows:, :].astype(F32)
        codes, gates = routing[:8], routing[8:]
        want, mask = tgt[...], lanemask[...]
        hit = jnp.zeros(tgt.shape, F32)
        gate = jnp.zeros(tgt.shape, F32)
        for k in range(8):
            same = codes[k : k + 1, :] == want
            hit = jnp.where(same, 1.0, hit)
            gate = jnp.where(same, gates[k : k + 1, :], gate)
        gate_col = jnp.sum(gate * mask, axis=1, keepdims=True)
        gate_cols[i, ab] = jnp.broadcast_to(gate_col, tgt.shape)
        wide = jnp.dot((hit * mask).astype(BF16), spread[...], preferred_element_type=F32)
        q_of = lax.broadcasted_iota(jnp.int32, (1, blk_rows), 1) % piece_rows // tok
        pick = jnp.concatenate(
            [jnp.where(q_of == q, wide, 0.0).astype(BF16) for q in range(q_n)], axis=0
        )
        got = jnp.dot(pick, blk[e], preferred_element_type=F32)
        got = jnp.concatenate(
            [got[q * 2 * rows_x : (q + 1) * 2 * rows_x] for q in range(q_n)], axis=1
        )
        return got.astype(BF16), (got * gate_col).astype(BF16)

    def compute(i):
        ea, eb = pair(i)
        rows_a, scaled_a = block_rows(ea, i, 0)
        rows_b, scaled_b = block_rows(eb, i, 1)
        parts = []
        for x in range(2):
            cut = slice(x * rows_x, (x + 1) * rows_x)
            scaled_rows[x, i, :rows_x, :] = scaled_a[cut]
            scaled_rows[x, i, rows_x:, :] = scaled_b[cut]
            lhs = jnp.concatenate([rows_a[cut], rows_b[cut]], axis=0)
            parts.append(
                jnp.dot(lhs[:, :fs], w2[0, x], preferred_element_type=F32)
                + jnp.dot(lhs[:, fs:], w2[1, x], preferred_element_type=F32)
            )
        for x in range(n_x):
            tiles = [
                parts[b][ab * rows_x + x * RPAD : ab * rows_x + (x + 1) * RPAD]
                for ab in range(2)
                for b in range(2)
            ]
            p_send[x, i] = jnp.concatenate(tiles, axis=0).astype(BF16)

    def p_copy(o, i):
        t = (xi + o) % n_x
        return remote(
            p_send.at[t, i], p_recv.at[xi, i], ps_send.at[o - 1, i], ps_recv.at[o - 1, i], x_dev(t)
        )

    def g_copy(o):
        t = (me + o) % n_e
        return remote(gs.at[t], gr.at[me], g_send.at[o], g_recv.at[o], {"expert": t})

    def combine(i):
        for o in range(1, n_x):
            p_copy(o, i).wait_recv()
        total = p_send[xi, i].astype(F32)
        for o in range(1, n_x):
            total = total + p_recv[(xi + n_x - o) % n_x, i].astype(F32)
        for ab in range(2):
            e = pair(i)[ab]
            part = total[ab * 16 : (ab + 1) * 16]
            gate = jnp.concatenate(
                [gate_cols[i, ab, pl.ds(pl.multiple_of(x * rows_x + xi * RPAD, RPAD), RPAD), :] for x in range(2)],
                axis=0,
            )
            hg_out[e] = (gate[:, :1] * part).astype(BF16)
            grad = jnp.sum(part * hp[e].astype(F32), axis=1, keepdims=True)
            r16 = lax.broadcasted_iota(jnp.int32, (16, LANES), 0)
            l16 = lax.broadcasted_iota(jnp.int32, (16, LANES), 1)
            line = jnp.where(l16 == r16, grad, 0.0)
            gs[e] = jnp.sum(line, axis=0, keepdims=True)

        g_copy(n_e - order(i)).start()

        @pl.when(i >= 1)
        def _():
            g_copy(order(jnp.maximum(i - 1, 0))).start()

    def grad_step(j):
        for x in range(2):
            lhs, rhs = [], []
            for u in range(2):
                i = 2 * j + u
                lhs.append(scaled_rows[x, i])
                for ab in range(2):
                    e = pair(i)[ab]
                    for s in range(n_x):
                        rhs.append(hidr[s, e].astype(F32)[x * RPAD : (x + 1) * RPAD])
            lhs = jnp.concatenate(lhs, axis=0)
            rhs = jnp.concatenate(rhs, axis=0).astype(BF16)
            acc[x] += lax.dot_general(lhs, rhs, (((0,), (0,)), ((), ())), preferred_element_type=F32)

    @pl.loop(0, half)
    def _(i):
        for c in range(PIECES):
            pass_on(0, order(i), c, half)

            @pl.when(i >= 1)
            def _():
                pass_on(1, order(jnp.maximum(i - 1, 0)), c, half - 1)

        compute(i)
        for o in range(1, n_x):
            p_copy(o, i).start()

        @pl.when(i >= half // 2)
        def _():
            combine(i - half // 2)

        @pl.when(i >= 3 * half // 4)
        def _():
            combine(i - half // 4)

        @pl.when(i == half // 2)
        def _():
            own_h.wait()
            for o in range(1, n_x):
                h_copy(o).wait_recv()

        @pl.when(i >= half // 2)
        def _():
            grad_step(i - half // 2)

    cut = fs // n_p

    def c_copy(x):
        return remote(ws.at[x], wc.at[x], c_send.at[x], c_recv.at[x], other)

    def r_copy(o, x):
        t = (p + o) % n_p
        return remote(wd.at[t, x], wr.at[p, x], r_send.at[o - 1, x], r_recv.at[o - 1, x], {"dp": t})

    def a_copy(o, x, src):
        at = wag.at[src, x]
        return remote(at, at, a_send.at[o - 1, x], a_recv.at[o - 1, x], {"dp": (p + o) % n_p})

    def summed(t, x):
        at = pl.multiple_of(core * fs + t * cut, cut)
        return acc[x, pl.ds(at, cut), :] + wc[x, pl.ds(pl.multiple_of(t * cut, cut), cut), :].astype(F32)

    for x in range(2):
        ws[x] = acc[x, pl.ds(pl.multiple_of((1 - core) * fs, fs), fs), :].astype(BF16)
        c_copy(x).start()
    for x in range(2):
        c_copy(x).wait_recv()
        for o in range(1, n_p):
            t = (p + o) % n_p
            wd[t, x] = summed(t, x).astype(BF16)
            r_copy(o, x).start()

    @pl.loop(3 * half // 4, half)
    def _(i):
        combine(i)

    gr[me] = gs[me]
    for x in range(2):
        mine = summed(p, x)
        for o in range(1, n_p):
            r_copy(o, x).wait_recv()
            mine = mine + wr[(p + n_p - o) % n_p, x].astype(F32)
        wag[p, x] = mine.astype(BF16)
        for o in range(1, n_p):
            a_copy(o, x, p).start()

    @pl.loop(1, n_e)
    def _(o):
        g_copy(o).wait_recv()

    own = codes_own[...].astype(jnp.int32)
    e_of = lax.broadcasted_iota(jnp.int32, (n_e, LANES), 0)
    one = jnp.concatenate(
        [jnp.where(e_of == own[k : k + 1] // 16, 1.0, 0.0) for k in range(8)], axis=1
    )
    got = lax.dot_general(
        gr[:, 0, :], one, (((0,), (0,)), ((), ())),
        preferred_element_type=F32, precision=lax.Precision.HIGHEST,
    )[:16]
    s_of = lax.broadcasted_iota(jnp.int32, (16, LANES), 0)
    lines = [
        jnp.sum(
            jnp.where(s_of == own[k : k + 1] % 16, got[:, k * LANES : (k + 1) * LANES], 0.0),
            axis=0, keepdims=True,
        )
        for k in range(8)
    ]
    gg_out[...] = lax.dot_general(
        jnp.concatenate(lines, axis=0), place, (((1,), (1,)), ((), ())),
        preferred_element_type=F32, precision=lax.Precision.HIGHEST,
    )

    for x in range(2):
        wg_out[x, pl.ds(pl.multiple_of(p * cut, cut), cut), :] = wag[p, x].astype(F32)
        for o in range(1, n_p):
            src = (p + n_p - o) % n_p
            a_copy(o, x, src).wait_recv()
            wg_out[x, pl.ds(pl.multiple_of(src * cut, cut), cut), :] = wag[src, x].astype(F32)

    for o in range(1, n_x):
        x_copy(o).wait_send()
        t_copy(o).wait_send()
        h_copy(o).wait_send()
    w_copy.wait_send()
    for x in range(2):
        c_copy(x).wait_send()
        for o in range(1, n_p):
            r_copy(o, x).wait_send()
            a_copy(o, x, p).wait_send()

    @pl.loop(1, n_e)
    def _(o):
        g_copy(o).wait_send()

    @pl.loop(0, half)
    def _(i):
        for o in range(1, n_x):
            p_copy(o, i).wait_send()
        for c in range(PIECES):
            hop(0, me, i + 1, c, 1).wait_send()

            @pl.when(i < half - 1)
            def _():
                hop(1, me, i + 1, c, 1).wait_send()


def shards(n_e, n_x, n_p, out_grad, gates, routes, hidden_acts, w_down):
    tok, top = routes.shape
    exp_dev = w_down.shape[1]
    fs = w_down.shape[0]
    width = w_down.shape[2]
    slot = hidden_acts.shape[1] // n_e
    half = n_e // 2
    chip_cols = 2 * fs
    q_n = chip_cols // LANES
    piece_rows = q_n * tok
    blk_rows = n_x * piece_rows + 16
    rows_x = n_x * RPAD

    pre = out_grad.reshape(tok, n_x, q_n, LANES).transpose(1, 2, 0, 3).reshape(n_x, piece_rows, LANES)
    hp = hidden_acts.reshape(exp_dev, n_e, slot, width).transpose(1, 0, 2, 3)
    hp = jnp.pad(hp, ((0, 0), (0, 0), (0, RPAD - slot), (0, 0))).reshape(n_e, 2 * RPAD, width)
    wt = w_down.transpose(1, 0, 2)

    dma = pltpu.SemaphoreType.DMA
    vmem = pl.BlockSpec(memory_space=pltpu.VMEM)
    cut = fs // n_p
    hg, gg, wg = pl.pallas_call(
        functools.partial(kernel, n_e, n_x, n_p, tok),
        out_shape=(
            jax.ShapeDtypeStruct((n_e, 2 * RPAD, width), BF16),
            jax.ShapeDtypeStruct((top, tok), F32),
            jax.ShapeDtypeStruct((exp_dev, fs, width), F32),
        ),
        in_specs=[vmem] * 5,
        out_specs=(vmem,) * 3,
        scratch_shapes=[
            pltpu.VMEM((n_e, blk_rows, LANES), BF16),
            pltpu.VMEM((n_x, piece_rows, LANES), BF16),
            pltpu.VMEM((16, LANES), BF16),
            pltpu.VMEM((n_x, 16, LANES), BF16),
            pltpu.VMEM((8, LANES), F32),
            pltpu.VMEM((n_x, n_e, 2 * RPAD, width), BF16),
            pltpu.VMEM((2, exp_dev, fs, width), BF16),
            pltpu.VMEM((LANES, blk_rows), BF16),
            pltpu.VMEM((2 * rows_x, LANES), F32),
            pltpu.VMEM((2 * rows_x, LANES), F32),
            pltpu.VMEM((n_x, half, 4 * RPAD, width), BF16),
            pltpu.VMEM((n_x, half, 4 * RPAD, width), BF16),
            pltpu.VMEM((2, half, 2 * rows_x, chip_cols), BF16),
            pltpu.VMEM((half, 2, 2 * rows_x, LANES), F32),
            pltpu.VMEM((2, chip_cols, width), F32),
            pltpu.VMEM((n_e, 1, LANES), F32),
            pltpu.VMEM((n_e, 1, LANES), F32),
            pltpu.VMEM((2, fs, width), BF16),
            pltpu.VMEM((2, fs, width), BF16),
            pltpu.VMEM((n_p, 2, cut, width), BF16),
            pltpu.VMEM((n_p, 2, cut, width), BF16),
            pltpu.VMEM((n_p, 2, cut, width), BF16),
            dma((n_x - 1,)), dma((n_x - 1,)), dma((n_x - 1,)), dma((n_x - 1,)), dma((n_x - 1,)), dma((n_x - 1,)),
            dma, dma, dma((3,)),
            dma((2, half, PIECES)), dma((2, half, PIECES)),
            dma((n_x - 1, half)), dma((n_x - 1, half)),
            dma((n_e,)), dma((n_e,)), dma((2,)), dma((2,)),
            dma((n_p - 1, 2)), dma((n_p - 1, 2)), dma((n_p - 1, 2)), dma((n_p - 1, 2)),
        ],
        compiler_params=pltpu.CompilerParams(
            collective_id=0, has_side_effects=True, vmem_limit_bytes=40 * 1024 * 1024
        ),
    )(pre, routes.T, gates.T, hp, wt)
    hg = hg.reshape(n_e, exp_dev, RPAD, width)[:, :, :slot].transpose(1, 0, 2, 3)
    return hg.reshape(exp_dev, n_e * slot, width), gg.T, wg.transpose(1, 0, 2)


def solution(mesh):
    n_x = mesh.shape["fsdp"] // 2
    in_specs = (
        P(("expert", "fsdp", "dp"), None),
        P(("expert", "fsdp", "dp"), None),
        P(("expert", "fsdp", "dp"), None),
        P("expert", ("fsdp", "dp"), None),
        P("fsdp", "expert", None),
    )
    out_specs = (
        P("expert", ("fsdp", "dp"), None),
        P(("expert", "fsdp", "dp"), None),
        P("fsdp", "expert", None),
    )
    return jax.shard_map(
        functools.partial(shards, mesh.shape["expert"], n_x, mesh.shape["dp"]),
        mesh=mesh,
        in_specs=in_specs,
        out_specs=out_specs,
        check_vma=False,
    )
```

time: 129 us -> 110 us (0.85); the launches traced: 129 us -> 109 us
  Pallas kernels: 118 us -> 102 us
  other arithmetic: 3.38 us -> 0 us
    pallas_call x1, Pallas kernels: 118 us -> 102 us  [shards(): pl.pallas_call(functools.partial(kernel, n_e, n_x, n_p, tok), out_shape=(...]
    reduce_sum x1 -> x0, other arithmetic: 3.16 us -> none  [shards(): jnp.sum((same & earlier[:, None, :, None]).astype(jnp.int32), axis=(2, 3))]
    unnamed x18 -> x15, local copies, waits for them, and re-layouts: 6.63 us -> 5.07 us
where the time goes in v2:
time: 110 us; the launch traced here: 109 us
  Pallas kernels  102 us (93%)
  local copies, waits for them, and re-layouts  6.17 us (6%)
    pallas_call x1, Pallas kernels, shards(): pl.pallas_call(functools.partial(kernel, n_e, n_x, n_p, tok), out_shape=(...  102 us
    unnamed x15, local copies, waits for them, and re-layouts  5.07 us

profile of v2, /device:TPU:6, one launch (start us, length us, event | category | flops | bytes accessed | tf_op | source)
XLA Modules:
  0.0 108.7 jit_solution(14886505114019595177)
XLA Ops:
  0.6 0.0 copy-start.3
  0.6 1.0 reshape.24
  1.7 0.0 copy-done.3
  1.7 0.3 copy.14
  2.0 0.1 copy.22
  2.0 0.0 copy-start.2
  2.0 0.1 pad_bitcast_fusion.hp
  2.1 0.9 copy-done.2
  3.0 0.0 copy-start
  3.0 0.0 copy-start.1
  3.1 0.6 copy-done
  3.7 0.0 copy-done.1
  3.7 101.8 %shard_map.76 = (bf16[32,16,384]{2,1,0:T(8,128)(2,1)S(1)}, f32[8,20]{1,0:T(8,128)S(1)}, f32[2,256,384]{2,1,0:T(8,128)S(1)}) custom-call(bf16[4,80,128]{2,1,0:T(8,128)(2,1)S(1)} %copy.17.pre, s32[8,20]{1,0:T(8,128)S(1)} %bitcast.23, f32[8,20]{1,0:T(8,128)S(1)} %bitcast.24, bf16[32,16,384]{2,1,0:T(8,128)(2,1)S(1)} %pad_bitcast_fusion.hp, ...), custom_call_target="tpu_custom_call" | custom-call | tf_op jit(solution)/shard_map/pallas_call | solution.py:421
  105.6 0.3 copy.21
  105.8 0.8 copy.19
  106.6 1.5 %copy.20 = f32[256,2,384]{2,1,0:T(2,128)} copy(f32[256,2,384]{2,0,1:T(8,128)S(1)} %bitcast.21) | data formatting | bytes 1572864
  108.1 0.6 copy.26
  (3 shorter events, 0.1 us)
Async XLA Ops:
  0.6 1.1 copy-start.3
  2.0 1.0 copy-start.2
  3.0 0.7 copy-start
  3.0 0.7 copy-start.1

commit v3 on v2

--- a/solution.py
+++ b/solution.py
@@ -14,13 +14,17 @@
 RPAD = 8
 CODE_SHIFT = 256.0
 PIECES = 3
-JUMP = 6
+JUMP = 4
 
 
 def remote(src, dst, send, recv, where):
     return pltpu.make_async_remote_copy(
         src_ref=src, dst_ref=dst, send_sem=send, recv_sem=recv, device_id=where, device_id_type=MESH
     )
+
+
+def wrap(v, n):
+    return jnp.where(v >= n, v - n, v)
 
 
 def kernel(
@@ -29,7 +33,7 @@
     blk, xr, tile, tr, codes_own, hidr, w2, spread, tgt, lanemask, p_send, p_recv, scaled_rows, gate_cols, acc,
     gs, gr, ws, wc, wd, wr, wag,
     x_send, x_recv, t_send, t_recv, h_send, h_recv, w_send, w_recv, loc,
-    z_send, z_recv, ps_send, ps_recv, g_send, g_recv, c_send, c_recv, r_send, r_recv, a_send, a_recv,
+    z_send, z_recv, d_send, d_recv, o_send, o_recv, ps_send, ps_recv, g_send, g_recv, c_send, c_recv, r_send, r_recv, a_send, a_recv,
 ):
     me = lax.axis_index("expert")
     f = lax.axis_index("fsdp")
@@ -53,24 +57,24 @@
     barrier = pltpu.get_barrier_semaphore()
 
     for o in (1, n_e - 1, JUMP, n_e - JUMP):
-        pl.semaphore_signal(barrier, inc=1, device_id={"expert": (me + o) % n_e}, device_id_type=MESH)
+        pl.semaphore_signal(barrier, inc=1, device_id={"expert": wrap(me + o, n_e)}, device_id_type=MESH)
     for o in range(1, n_x):
-        pl.semaphore_signal(barrier, inc=1, device_id=x_dev((xi + o) % n_x), device_id_type=MESH)
+        pl.semaphore_signal(barrier, inc=1, device_id=x_dev(wrap(xi + o, n_x)), device_id_type=MESH)
     pl.semaphore_signal(barrier, inc=1, device_id=other, device_id_type=MESH)
     for o in range(1, n_p):
-        pl.semaphore_signal(barrier, inc=1, device_id={"dp": (p + o) % n_p}, device_id_type=MESH)
+        pl.semaphore_signal(barrier, inc=1, device_id={"dp": wrap(p + o, n_p)}, device_id_type=MESH)
     pl.semaphore_wait(barrier, 4 + (n_x - 1) + 1 + (n_p - 1))
 
     def x_copy(o):
-        t = (xi + o) % n_x
+        t = wrap(xi + o, n_x)
         return remote(pre.at[t], xr.at[xi], x_send.at[o - 1], x_recv.at[o - 1], x_dev(t))
 
     def t_copy(o):
-        t = (xi + o) % n_x
+        t = wrap(xi + o, n_x)
         return remote(tile, tr.at[xi], t_send.at[o - 1], t_recv.at[o - 1], x_dev(t))
 
     def h_copy(o):
-        t = (xi + o) % n_x
+        t = wrap(xi + o, n_x)
         return remote(hp, hidr.at[xi], h_send.at[o - 1], h_recv.at[o - 1], x_dev(t))
 
     w_copy = remote(wt, w2.at[core], w_send, w_recv, other)
@@ -133,35 +137,58 @@
         t_copy(o).wait_recv()
     table = jnp.zeros((16, LANES), F32)
     for x in range(n_x):
-        blk[me, x * piece_rows : (x + 1) * piece_rows, :] = xr[x]
+        blk[core, me, x * piece_rows : (x + 1) * piece_rows, :] = xr[x]
         table = table + tr[x].astype(F32)
-    blk[me, og_rows:, :] = table.astype(BF16)
-
-    def hop(way, slot, dist, c, stride):
-        ref = blk.at[slot, pl.ds(c * chunk, chunk), :]
-        to = (me + stride) % n_e if way == 0 else (me + n_e - stride) % n_e
-        return remote(ref, ref, z_send.at[way, dist - 1, c], z_recv.at[way, dist - 1, c], {"expert": to})
+    blk[core, me, og_rows:, :] = table.astype(BF16)
+
+    def hop(h, slot, dist, c, stride):
+        ref = blk.at[h, slot, pl.ds(c * chunk, chunk), :]
+        to = wrap(me + jnp.where(core == 0, stride, n_e - stride), n_e)
+        return remote(ref, ref, z_send.at[h, dist - 1, c], z_recv.at[h, dist - 1, c], {"expert": to})
 
     def seen(way, dist):
-        return (me + n_e - dist) % n_e if way == 0 else (me + dist) % n_e
+        return wrap(me + jnp.where(way == 0, n_e - dist, dist), n_e)
+
+    def hand_over(slot, i):
+        ref = blk.at[1 - core, slot]
+        return remote(ref, ref, d_send.at[i], d_recv.at[i], other)
+
+    def handed(slot, i):
+        ref = blk.at[core, slot]
+        return remote(ref, ref, d_send.at[i], d_recv.at[i], other)
+
+    own_half = blk.at[core, me]
+    o_copy = remote(own_half, own_half, o_send, o_recv, other)
+    their_half = blk.at[1 - core, me]
+    o_arrival = remote(their_half, their_half, o_send, o_recv, other)
+    last = half - core
 
     def order(i):
         mid = jnp.where(i % 2 == 0, JUMP - 1 + i // 2, (i + 3) // 2)
         return jnp.where((i < 2) | (i >= 2 * JUMP - 4), i + 1, mid)
 
+    o_copy.start()
     for c in range(PIECES):
-        for way in range(2):
-            hop(way, me, 1, c, 1).start()
+        hop(core, me, 1, c, 1).start()
+    o_arrival.wait_recv()
     for c in range(PIECES):
-        for way in range(2):
-            hop(way, me, JUMP, c, JUMP).start()
-
-    def pass_on(way, dist, c, last):
-        hop(way, seen(way, dist), dist, c, 1).wait_recv()
-
-        @pl.when((dist != JUMP - 1) & (dist != last))
-        def _():
-            hop(way, seen(way, dist), dist + 1, c, 1).start()
+        hop(1 - core, me, 1, c, 1).start()
+    for h in range(2):
+        for c in range(PIECES):
+            hop(h, me, JUMP, c, JUMP).start()
+
+    def pass_on(dist, i):
+        slot = seen(core, dist)
+        more = (dist != JUMP - 1) & (dist != last)
+        for h in (core, 1 - core):
+            for c in range(PIECES):
+                hop(h, slot, dist, c, 1).wait_recv()
+
+                @pl.when(more)
+                def _():
+                    hop(h, slot, dist + 1, c, 1).start()
+
+        hand_over(slot, i).start()
 
     def pair(i):
         far = jnp.where(i >= 1, order(jnp.maximum(i - 1, 0)), 0)
@@ -171,7 +198,7 @@
     w_copy.wait_recv()
 
     def block_rows(e, i, ab):
-        routing = blk[e, og_rows:, :].astype(F32)
+        routing = blk[core, e, og_rows:, :].astype(F32)
         codes, gates = routing[:8], routing[8:]
         want, mask = tgt[...], lanemask[...]
         hit = jnp.zeros(tgt.shape, F32)
@@ -187,7 +214,7 @@
         pick = jnp.concatenate(
             [jnp.where(q_of == q, wide, 0.0).astype(BF16) for q in range(q_n)], axis=0
         )
-        got = jnp.dot(pick, blk[e], preferred_element_type=F32)
+        got = jnp.dot(pick, blk[core, e], preferred_element_type=F32)
         got = jnp.concatenate(
             [got[q * 2 * rows_x : (q + 1) * 2 * rows_x] for q in range(q_n)], axis=1
         )
@@ -216,13 +243,13 @@
             p_send[x, i] = jnp.concatenate(tiles, axis=0).astype(BF16)
 
     def p_copy(o, i):
-        t = (xi + o) % n_x
+        t = wrap(xi + o, n_x)
         return remote(
             p_send.at[t, i], p_recv.at[xi, i], ps_send.at[o - 1, i], ps_recv.at[o - 1, i], x_dev(t)
         )
 
     def g_copy(o):
-        t = (me + o) % n_e
+        t = wrap(me + o, n_e)
         return remote(gs.at[t], gr.at[me], g_send.at[o], g_recv.at[o], {"expert": t})
 
     def combine(i):
@@ -230,7 +257,7 @@
             p_copy(o, i).wait_recv()
         total = p_send[xi, i].astype(F32)
         for o in range(1, n_x):
-            total = total + p_recv[(xi + n_x - o) % n_x, i].astype(F32)
+            total = total + p_recv[wrap(xi + n_x - o, n_x), i].astype(F32)
         for ab in range(2):
             e = pair(i)[ab]
             part = total[ab * 16 : (ab + 1) * 16]
@@ -265,14 +292,16 @@
             rhs = jnp.concatenate(rhs, axis=0).astype(BF16)
             acc[x] += lax.dot_general(lhs, rhs, (((0,), (0,)), ((), ())), preferred_element_type=F32)
 
-    @pl.loop(0, half)
-    def _(i):
-        for c in range(PIECES):
-            pass_on(0, order(i), c, half)
-
-            @pl.when(i >= 1)
-            def _():
-                pass_on(1, order(jnp.maximum(i - 1, 0)), c, half - 1)
+    def work(i):
+        ea, eb = pair(i)
+
+        @pl.when(core == 1)
+        def _():
+            handed(eb, i).wait_recv()
+
+        @pl.when((core == 0) & (i >= 1))
+        def _():
+            handed(ea, i - 1).wait_recv()
 
         compute(i)
         for o in range(1, n_x):
@@ -296,18 +325,30 @@
         def _():
             grad_step(i - half // 2)
 
+    @pl.loop(0, half)
+    def _(i):
+        @pl.when(i < last)
+        def _():
+            pass_on(order(i), i)
+
+        @pl.when(i >= 1)
+        def _():
+            work(i - 1)
+
+    work(half - 1)
+
     cut = fs // n_p
 
     def c_copy(x):
         return remote(ws.at[x], wc.at[x], c_send.at[x], c_recv.at[x], other)
 
     def r_copy(o, x):
-        t = (p + o) % n_p
+        t = wrap(p + o, n_p)
         return remote(wd.at[t, x], wr.at[p, x], r_send.at[o - 1, x], r_recv.at[o - 1, x], {"dp": t})
 
     def a_copy(o, x, src):
         at = wag.at[src, x]
-        return remote(at, at, a_send.at[o - 1, x], a_recv.at[o - 1, x], {"dp": (p + o) % n_p})
+        return remote(at, at, a_send.at[o - 1, x], a_recv.at[o - 1, x], {"dp": wrap(p + o, n_p)})
 
     def summed(t, x):
         at = pl.multiple_of(core * fs + t * cut, cut)
@@ -316,23 +357,24 @@
     for x in range(2):
         ws[x] = acc[x, pl.ds(pl.multiple_of((1 - core) * fs, fs), fs), :].astype(BF16)
         c_copy(x).start()
+
+    @pl.loop(3 * half // 4, half)
+    def _(i):
+        combine(i)
+
+    gr[me] = gs[me]
     for x in range(2):
         c_copy(x).wait_recv()
         for o in range(1, n_p):
-            t = (p + o) % n_p
+            t = wrap(p + o, n_p)
             wd[t, x] = summed(t, x).astype(BF16)
             r_copy(o, x).start()
 
-    @pl.loop(3 * half // 4, half)
-    def _(i):
-        combine(i)
-
-    gr[me] = gs[me]
     for x in range(2):
         mine = summed(p, x)
         for o in range(1, n_p):
             r_copy(o, x).wait_recv()
-            mine = mine + wr[(p + n_p - o) % n_p, x].astype(F32)
+            mine = mine + wr[wrap(p + n_p - o, n_p), x].astype(F32)
         wag[p, x] = mine.astype(BF16)
         for o in range(1, n_p):
             a_copy(o, x, p).start()
@@ -366,7 +408,7 @@
     for x in range(2):
         wg_out[x, pl.ds(pl.multiple_of(p * cut, cut), cut), :] = wag[p, x].astype(F32)
         for o in range(1, n_p):
-            src = (p + n_p - o) % n_p
+            src = wrap(p + n_p - o, n_p)
             a_copy(o, x, src).wait_recv()
             wg_out[x, pl.ds(pl.multiple_of(src * cut, cut), cut), :] = wag[src, x].astype(F32)
 
@@ -389,12 +431,15 @@
     def _(i):
         for o in range(1, n_x):
             p_copy(o, i).wait_send()
-        for c in range(PIECES):
-            hop(0, me, i + 1, c, 1).wait_send()
-
-            @pl.when(i < half - 1)
-            def _():
-                hop(1, me, i + 1, c, 1).wait_send()
+
+        @pl.when(i < last)
+        def _():
+            hand_over(me, i).wait_send()
+            for h in range(2):
+                for c in range(PIECES):
+                    hop(h, me, i + 1, c, 1).wait_send()
+
+    o_copy.wait_send()
 
 
 def shards(n_e, n_x, n_p, out_grad, gates, routes, hidden_acts, w_down):
@@ -428,7 +473,7 @@
         in_specs=[vmem] * 5,
         out_specs=(vmem,) * 3,
         scratch_shapes=[
-            pltpu.VMEM((n_e, blk_rows, LANES), BF16),
+            pltpu.VMEM((2, n_e, blk_rows, LANES), BF16),
             pltpu.VMEM((n_x, piece_rows, LANES), BF16),
             pltpu.VMEM((16, LANES), BF16),
             pltpu.VMEM((n_x, 16, LANES), BF16),
@@ -452,7 +497,7 @@
             pltpu.VMEM((n_p, 2, cut, width), BF16),
             dma((n_x - 1,)), dma((n_x - 1,)), dma((n_x - 1,)), dma((n_x - 1,)), dma((n_x - 1,)), dma((n_x - 1,)),
             dma, dma, dma((3,)),
-            dma((2, half, PIECES)), dma((2, half, PIECES)),
+            dma((2, half, PIECES)), dma((2, half, PIECES)), dma((half,)), dma((half,)), dma, dma,
             dma((n_x - 1, half)), dma((n_x - 1, half)),
             dma((n_e,)), dma((n_e,)), dma((2,)), dma((2,)),
             dma((n_p - 1, 2)), dma((n_p - 1, 2)), dma((n_p - 1, 2)), dma((n_p - 1, 2)),

time: 110 us -> 115 us (1.045)
  the two profiles are of different devices: /device:TPU:6 before, /device:TPU:2 now
where the time goes in v3:
time: 115 us
  Pallas kernels  108 us (94%)
  local copies, waits for them, and re-layouts  6.17 us (5%)
    pallas_call x1, Pallas kernels, shards(): pl.pallas_call(functools.partial(kernel, n_e, n_x, n_p, tok), out_shape=(...  108 us
    unnamed x15, local copies, waits for them, and re-layouts  5.07 us

profile of v3, /device:TPU:2, one launch (start us, length us, event | category | flops | bytes accessed | tf_op | source)
XLA Modules:
  0.0 114.5 jit_solution(16731892220229848066)
XLA Ops:
  0.6 0.0 copy-start.3
  0.6 1.0 reshape.24
  1.7 0.0 copy-done.3
  1.7 0.3 copy.14
  2.0 0.1 copy.22
  2.0 0.0 copy-start.2
  2.0 0.1 pad_bitcast_fusion.hp
  2.1 0.9 copy-done.2
  3.0 0.0 copy-start
  3.0 0.0 copy-start.1
  3.1 0.6 copy-done
  3.7 0.0 copy-done.1
  3.7 107.7 %shard_map.76 = (bf16[32,16,384]{2,1,0:T(8,128)(2,1)S(1)}, f32[8,20]{1,0:T(8,128)S(1)}, f32[2,256,384]{2,1,0:T(8,128)S(1)}) custom-call(bf16[4,80,128]{2,1,0:T(8,128)(2,1)S(1)} %copy.17.pre, s32[8,20]{1,0:T(8,128)S(1)} %bitcast.23, f32[8,20]{1,0:T(8,128)S(1)} %bitcast.24, bf16[32,16,384]{2,1,0:T(8,128)(2,1)S(1)} %pad_bitcast_fusion.hp, ...), custom_call_target="tpu_custom_call" | custom-call | tf_op jit(solution)/shard_map/pallas_call | solution.py:466
  111.4 0.3 copy.21
  111.7 0.8 copy.19
  112.5 1.5 %copy.20 = f32[256,2,384]{2,1,0:T(2,128)} copy(f32[256,2,384]{2,0,1:T(8,128)S(1)} %bitcast.21) | data formatting | bytes 1572864
  114.0 0.6 copy.26
  (3 shorter events, 0.1 us)
Async XLA Ops:
  0.6 1.1 copy-start.3
  2.0 1.0 copy-start.2
  3.0 0.7 copy-start
  3.0 0.7 copy-start.1

commit v4 on v2

--- a/solution.py
+++ b/solution.py
@@ -14,7 +14,7 @@
 RPAD = 8
 CODE_SHIFT = 256.0
 PIECES = 3
-JUMP = 6
+JUMP = 8
 
 
 def remote(src, dst, send, recv, where):

time: 110 us -> 108 us (0.982)
  Pallas kernels: 102 us -> 100 us
    pallas_call x1, Pallas kernels: 102 us -> 100 us  [shards(): pl.pallas_call(functools.partial(kernel, n_e, n_x, n_p, tok), out_shape=(...]
where the time goes in v4:
time: 108 us; the launch traced here: 107 us
  Pallas kernels  100 us (93%)
  local copies, waits for them, and re-layouts  6.17 us (6%)
    pallas_call x1, Pallas kernels, shards(): pl.pallas_call(functools.partial(kernel, n_e, n_x, n_p, tok), out_shape=(...  100 us
    unnamed x15, local copies, waits for them, and re-layouts  5.07 us

profile of v4, /device:TPU:6, one launch (start us, length us, event | category | flops | bytes accessed | tf_op | source)
XLA Modules:
  0.0 106.9 jit_solution(17901585541822138524)
XLA Ops:
  0.6 0.0 copy-start.3
  0.6 1.0 reshape.24
  1.7 0.0 copy-done.3
  1.7 0.3 copy.14
  2.0 0.1 copy.22
  2.0 0.0 copy-start.2
  2.0 0.1 pad_bitcast_fusion.hp
  2.1 0.9 copy-done.2
  3.0 0.0 copy-start
  3.0 0.0 copy-start.1
  3.1 0.6 copy-done
  3.7 0.0 copy-done.1
  3.7 100.0 %shard_map.76 = (bf16[32,16,384]{2,1,0:T(8,128)(2,1)S(1)}, f32[8,20]{1,0:T(8,128)S(1)}, f32[2,256,384]{2,1,0:T(8,128)S(1)}) custom-call(bf16[4,80,128]{2,1,0:T(8,128)(2,1)S(1)} %copy.17.pre, s32[8,20]{1,0:T(8,128)S(1)} %bitcast.23, f32[8,20]{1,0:T(8,128)S(1)} %bitcast.24, bf16[32,16,384]{2,1,0:T(8,128)(2,1)S(1)} %pad_bitcast_fusion.hp, ...), custom_call_target="tpu_custom_call" | custom-call | tf_op jit(solution)/shard_map/pallas_call | solution.py:421
  103.8 0.3 copy.21
  104.1 0.8 copy.19
  104.8 1.5 %copy.20 = f32[256,2,384]{2,1,0:T(2,128)} copy(f32[256,2,384]{2,0,1:T(8,128)S(1)} %bitcast.21) | data formatting | bytes 1572864
  106.3 0.6 copy.26
  (3 shorter events, 0.1 us)
Async XLA Ops:
  0.6 1.1 copy-start.3
  2.0 1.0 copy-start.2
  3.0 0.7 copy-start
  3.0 0.7 copy-start.1
